TPU v7x, 256 devices: a whole 4x4x8 slice. The times are simulated.
256 devices in a mesh: gx: 16 (over y_lo, x, core), gy: 16 (over y_hi, z).
Axes of the slice: x: 4, y: 4 (y_hi: 2, y_lo: 2; y = y_hi * 2 + y_lo), z: 8, core: 2. Of those that a mesh axis runs over, the one named last changes fastest.
Arguments:
- labels: int32 [64, 256, 256], P('gx', 'gy'), may hold values from 0 to 7
- speed: float32 [8], replicated, may hold values from 0.9 to 2
- absorption: float32 [8], replicated, may hold values from 0.01 to 0.15
- amplitude: float32 [2, 16, 2], replicated, may hold values from -6 to 6
- source_x: int32 [2, 16], replicated, may hold values from 0 to 60
- source_y: int32 [2, 16], replicated, may hold values from 0 to 252
- source_z: int32 [2, 16], replicated, may hold values from 0 to 252
Outputs:
- field: float32 [2, 2, 64, 256, 256], P(None, None, 'gx', 'gy')
Inputs may be any that keep to these rules, and one draw needn't show every extreme that they name: `labels`: indexes speed and absorption. `source_x`: each source block of 4 cells lies inside the grid. `source_y`: each source block of 4 cells lies inside the grid. `source_z`: each source block of 4 cells lies inside the grid.
All inputs are finite; a program needn't handle non-finite values.
Results may differ from a plain program's by a relative error of at most 0.00013.
Values sent between devices are 32-bit elements; how exact they have to be, the bound alone decides.
A program may use at most 64 MiB of HBM per device.

v0:
```python
import math

import jax
import jax.numpy as jnp
from jax import lax
from jax.sharding import PartitionSpec as P

SBLK = 4
ITERS = 4


wave_number = 2.0 * math.pi / 6.0
highest = lax.Precision.HIGHEST


def with_halo(block, sides, width):
    for axis, dim in sides:
        count = lax.axis_size(axis)
        forward = [(i, i + 1) for i in range(count - 1)]
        forward.append((count - 1, 0))
        backward = [(target, source) for source, target in forward]
        low = lax.ppermute(
            lax.slice_in_dim(block, block.shape[dim] - width, None, axis=dim), axis, forward
        )
        high = lax.ppermute(lax.slice_in_dim(block, 0, width, axis=dim), axis, backward)
        block = jnp.concatenate([low, block, high], axis=dim)
    return block


def medium_table(speed, absorption):
    real_k = wave_number / speed
    table_real = real_k * real_k - absorption * absorption
    table_imag = 2.0 * real_k * absorption
    centre = 0.5 * (jnp.min(table_real) + jnp.max(table_real))
    spread = 1.05 * jnp.max(jnp.sqrt((table_real - centre) ** 2 + table_imag**2))
    return (table_real, table_imag, centre, spread)


def along(values, matrix, axis):
    if axis == 1:
        return jnp.einsum("fxyz,kx->fkyz", values, matrix, precision=highest)
    if axis == 2:
        return jnp.einsum("fxyz,ky->fxkz", values, matrix, precision=highest)
    return jnp.einsum("fxyz,kz->fxyk", values, matrix, precision=highest)


def dft_tables(length):
    index = jnp.arange(length, dtype=jnp.int32)
    phase = 2.0 * math.pi * (index[:, None] * index[None, :] % length).astype(jnp.float32) / length
    return (jnp.cos(phase), jnp.sin(phase))


def transform(data, axis, tables, sign):
    cosine_table, sine_table = tables
    real_part = data[:, 0]
    imag_part = data[:, 1]
    cos_real = along(real_part, cosine_table, axis)
    sin_real = along(real_part, sine_table, axis)
    cos_imag = along(imag_part, cosine_table, axis)
    sin_imag = along(imag_part, sine_table, axis)
    if sign < 0:
        return jnp.stack([cos_real + sin_imag, cos_imag - sin_real], axis=1)
    return jnp.stack([cos_real - sin_imag, cos_imag + sin_real], axis=1)


def squared_wave(index, length):
    folded = jnp.where(index < length // 2, index, index - length).astype(jnp.float32)
    wave = 2.0 * math.pi * folded / length
    return wave * wave


def green_parts(index_x, total_x, index_y, total_y, index_z, total_z, centre, spread):
    wave_sq = (
        squared_wave(index_x, total_x)[:, None, None]
        + squared_wave(index_y, total_y)[None, :, None]
    )
    wave_sq = wave_sq + squared_wave(index_z, total_z)[None, None, :]
    shifted = wave_sq - centre
    denom = shifted * shifted + spread * spread
    return (shifted / denom, spread / denom)


def apply_green(data, parts):
    green_real, green_imag = parts
    real_part = data[:, 0]
    imag_part = data[:, 1]
    return jnp.stack(
        [
            green_real * real_part - green_imag * imag_part,
            green_real * imag_part + green_imag * real_part,
        ],
        axis=1,
    )


def block_mask(corner, start, count):
    cells = start + jnp.arange(count, dtype=jnp.int32)
    inside = (cells[None, None, :] >= corner[:, :, None]) & (
        cells[None, None, :] < corner[:, :, None] + SBLK
    )
    return inside.astype(jnp.float32)


def per_device(labels, speed, absorption, amplitude, source_x, source_y, source_z):
    count_x, count_y, depth = labels.shape
    groups_x = lax.axis_size("gx")
    groups_y = lax.axis_size("gy")
    total_x = count_x * groups_x
    total_y = count_y * groups_y
    place_x = lax.axis_index("gx")
    place_y = lax.axis_index("gy")
    table_real, table_imag, centre, spread = medium_table(speed, absorption)
    classes = jnp.arange(speed.shape[0], dtype=jnp.int32)
    onehot = (labels[None] == classes[:, None, None, None]).astype(jnp.float32)
    local = jnp.einsum(
        "lxyz,cl->cxyz", onehot, jnp.stack([table_real, table_imag]), precision=highest
    )
    padded = with_halo(local, (("gx", 1), ("gy", 2)), 1)
    beside_all = (
        padded[:, 2:, 1:-1] + padded[:, :-2, 1:-1] + padded[:, 1:-1, 2:] + padded[:, 1:-1, :-2]
    )
    beside_all = beside_all + jnp.roll(local, 1, 3) + jnp.roll(local, -1, 3)
    smooth = 0.5 * local + beside_all / 12.0
    pot_real = smooth[0] - centre
    pot_imag = smooth[1] - spread
    gain_real = -pot_imag / spread
    gain_imag = pot_real / spread
    mask_x = block_mask(source_x, place_x * count_x, count_x)
    mask_y = block_mask(source_y, place_y * count_y, count_y)
    mask_z = block_mask(source_z, 0, depth)
    first = jnp.einsum("fsc,fsx->fcsx", amplitude, mask_x, precision=highest)
    second = jnp.einsum("fcsx,fsy->fcsxy", first, mask_y, precision=highest)
    source = jnp.einsum("fcsxy,fsz->fcxyz", second, mask_z, precision=highest)
    tables_x = dft_tables(total_x)
    tables_y = dft_tables(total_y)
    tables_z = dft_tables(depth)
    scale = 1.0 / (total_x * total_y * depth)
    index_x = place_y * (total_x // groups_y) + jnp.arange(total_x // groups_y, dtype=jnp.int32)
    index_y = jnp.arange(total_y, dtype=jnp.int32)
    index_z = place_x * (depth // groups_x) + jnp.arange(depth // groups_x, dtype=jnp.int32)
    parts = green_parts(index_x, total_x, index_y, total_y, index_z, depth, centre, spread)
    field = jnp.zeros_like(source)
    for iteration in range(ITERS):
        field_real = field[:, 0]
        field_imag = field[:, 1]
        rhs = (
            jnp.stack(
                [
                    pot_real * field_real - pot_imag * field_imag,
                    pot_real * field_imag + pot_imag * field_real,
                ],
                axis=1,
            )
            + source
        )
        spectra = transform(rhs, 3, tables_z, -1)
        spectra = transform(
            lax.all_to_all(spectra, "gx", split_axis=4, concat_axis=2, tiled=True), 1, tables_x, -1
        )
        spectra = transform(
            apply_green(
                transform(
                    lax.all_to_all(spectra, "gy", split_axis=2, concat_axis=3, tiled=True),
                    2,
                    tables_y,
                    -1,
                ),
                parts,
            ),
            2,
            tables_y,
            1,
        )
        spectra = transform(
            lax.all_to_all(spectra, "gy", split_axis=3, concat_axis=2, tiled=True), 1, tables_x, 1
        )
        scattered = (
            transform(
                lax.all_to_all(spectra, "gx", split_axis=2, concat_axis=4, tiled=True),
                3,
                tables_z,
                1,
            )
            * scale
        )
        change = scattered - field
        field = field + jnp.stack(
            [
                gain_real * change[:, 0] - gain_imag * change[:, 1],
                gain_real * change[:, 1] + gain_imag * change[:, 0],
            ],
            axis=1,
        )
    return field


def solution(mesh):
    return jax.shard_map(
        per_device,
        mesh=mesh,
        in_specs=(P("gx", "gy", None), P(), P(), P(), P(), P(), P()),
        out_specs=P(None, None, "gx", "gy", None),
        check_vma=False,
    )
```

profile of v0, /device:TPU:1, one launch (start us, length us, event | category | flops | bytes accessed | tf_op | source)
XLA Modules:
  0.0 510.0 jit_solution(14490123667051889105)
XLA Ops:
  5.2 2.7 collective-permute-start.1
  12.6 7.6 %collective-permute-start.2 = (f32[2,6,1,256]{3,0,2,1:T(2,128)S(1)}, f32[2,6,1,256]{3,0,2,1:T(2,128)S(1)}, u32[]{:S(2)}, u32[]{:S(2)}) collective-permute-start(f32[2,6,1,256]{3,0,2,1:T(2,128)S(1)} %get-tuple-element.40), channel_id=1, source_target_pairs={{1,0},{2,1},{3,2},{4,3},{5,4},{6,5},{7,6},{8,7},{9,8},{10,9},{11,1... | collective-permute-start | bytes 36872 | tf_op jit(solution)/shard_map/ppermute | solution.py:25
  21.5 4.8 collective-permute-done.3
  34.0 2.3 reshape.155
  36.3 7.7 %all-to-all-start = ((f32[16,1,4096]{2,1,0:T(1,128)}), f32[16,1,4096]{2,1,0:T(1,128)S(1)}, u32[]{:S(2)}, u32[]{:S(2)}) async-start(f32[16,1,4096]{2,1,0:T(1,128)} %reshape.155), calls=%async_computation | async-start | bytes 524288 | tf_op jit(solution)/shard_map/all_to_all | solution.py:158
  44.0 7.2 %all-to-all-done = f32[16,1,4096]{2,1,0:T(1,128)S(1)} async-done(((f32[16,1,4096]{2,1,0:T(1,128)}), f32[16,1,4096]{2,1,0:T(1,128)S(1)}, u32[]{:S(2)}, u32[]{:S(2)}) %all-to-all-start) | async-done | bytes 262176 | tf_op jit(solution)/shard_map/all_to_all | solution.py:158
  52.9 2.8 reshape.156
  55.7 1.9 copy.65
  59.2 1.7 copy.136
  63.4 1.8 copy.68
  66.7 3.5 all-to-all-start.1
  71.7 8.8 %all-to-all-done.1 = f32[16,1,4096]{2,1,0:T(1,128)S(1)} async-done(((f32[16,1,4096]{2,1,0:T(1,128)}), f32[16,1,4096]{2,1,0:T(1,128)S(1)}, u32[]{:S(2)}, u32[]{:S(2)}) %all-to-all-start.1) | async-done | bytes 262176 | tf_op jit(solution)/shard_map/all_to_all | solution.py:163
  82.4 2.0 copy.70
  84.4 2.7 all_to_all.215
  98.2 1.7 copy.71
  101.5 14.7 %all_to_all.288 = f32[16,1,4096]{2,1,0:T(1,128)S(1)} all-to-all(f32[16,1,4096]{2,1,0:T(1,128)S(1)} %reshape.159), channel_id=1, replica_groups=mesh['gx'=16,'gy'=16] {'gy'}, dimensions={0} | all-to-all | bytes 524288 | tf_op jit(solution)/shard_map/all_to_all | solution.py:175
  122.6 1.8 copy.75
  125.9 6.6 %all-to-all-start.3 = ((f32[16,1,4096]{2,1,0:T(1,128)}), f32[16,1,4096]{2,1,0:T(1,128)S(1)}, u32[]{:S(2)}, u32[]{:S(2)}) async-start(f32[16,1,4096]{2,1,0:T(1,128)} %reshape.161), calls=%async_computation.3 | async-start | bytes 524288 | tf_op jit(solution)/shard_map/all_to_all | solution.py:179
  132.5 7.1 %all-to-all-done.3 = f32[16,1,4096]{2,1,0:T(1,128)S(1)} async-done(((f32[16,1,4096]{2,1,0:T(1,128)}), f32[16,1,4096]{2,1,0:T(1,128)S(1)}, u32[]{:S(2)}, u32[]{:S(2)}) %all-to-all-start.3) | async-done | bytes 262176 | tf_op jit(solution)/shard_map/all_to_all | solution.py:179
  141.6 2.6 copy.77
  144.1 2.6 all_to_all.223
  160.9 10.5 %all_to_all.289 = f32[16,1,4096]{2,1,0:T(1,128)S(1)} all-to-all(f32[16,1,4096]{2,1,0:T(1,128)S(1)} %reshape.163), channel_id=1, replica_groups=mesh['gx'=16,'gy'=16] {'gx'}, dimensions={0} | all-to-all | bytes 524288 | tf_op jit(solution)/shard_map/all_to_all | solution.py:158
  172.5 2.8 reshape.164
  175.4 1.9 copy.79
  178.8 1.7 copy.140
  183.1 1.8 copy.82
  185.7 14.0 %all_to_all.290 = f32[16,1,4096]{2,1,0:T(1,128)S(1)} all-to-all(f32[16,1,4096]{2,1,0:T(1,128)S(1)} %reshape.165), channel_id=1, replica_groups=mesh['gx'=16,'gy'=16] {'gy'}, dimensions={0} | all-to-all | bytes 524288 | tf_op jit(solution)/shard_map/all_to_all | solution.py:163
  201.6 2.0 copy.84
  203.6 2.8 all_to_all.231
  219.1 1.6 reshape.167
  220.6 15.4 %all_to_all.291 = f32[16,1,4096]{2,1,0:T(1,128)S(1)} all-to-all(f32[16,1,4096]{2,1,0:T(1,128)S(1)} %reshape.167), channel_id=1, replica_groups=mesh['gx'=16,'gy'=16] {'gy'}, dimensions={0} | all-to-all | bytes 524288 | tf_op jit(solution)/shard_map/all_to_all | solution.py:175
  242.6 1.8 copy.89
  245.1 13.5 %all_to_all.292 = f32[16,1,4096]{2,1,0:T(1,128)S(1)} all-to-all(f32[16,1,4096]{2,1,0:T(1,128)S(1)} %reshape.169), channel_id=1, replica_groups=mesh['gx'=16,'gy'=16] {'gx'}, dimensions={0} | all-to-all | bytes 524288 | tf_op jit(solution)/shard_map/all_to_all | solution.py:179
  260.6 2.6 copy.91
  263.1 2.7 all_to_all.239
  276.9 1.7 copy.92
  280.2 10.5 %all_to_all.293 = f32[16,1,4096]{2,1,0:T(1,128)S(1)} all-to-all(f32[16,1,4096]{2,1,0:T(1,128)S(1)} %reshape.171), channel_id=1, replica_groups=mesh['gx'=16,'gy'=16] {'gx'}, dimensions={0} | all-to-all | bytes 524288 | tf_op jit(solution)/shard_map/all_to_all | solution.py:158
  291.8 2.8 reshape.172
  294.7 1.9 copy.93
  298.1 1.7 copy.144
  302.4 1.8 copy.96
  305.0 13.5 %all_to_all.294 = f32[16,1,4096]{2,1,0:T(1,128)S(1)} all-to-all(f32[16,1,4096]{2,1,0:T(1,128)S(1)} %reshape.173), channel_id=1, replica_groups=mesh['gx'=16,'gy'=16] {'gy'}, dimensions={0} | all-to-all | bytes 524288 | tf_op jit(solution)/shard_map/all_to_all | solution.py:163
  320.3 2.0 copy.98
  322.4 2.6 all_to_all.247
  337.6 1.6 reshape.175
  339.2 15.4 %all_to_all.295 = f32[16,1,4096]{2,1,0:T(1,128)S(1)} all-to-all(f32[16,1,4096]{2,1,0:T(1,128)S(1)} %reshape.175), channel_id=1, replica_groups=mesh['gx'=16,'gy'=16] {'gy'}, dimensions={0} | all-to-all | bytes 524288 | tf_op jit(solution)/shard_map/all_to_all | solution.py:175
  361.1 1.8 copy.103
  363.7 13.5 %all_to_all.296 = f32[16,1,4096]{2,1,0:T(1,128)S(1)} all-to-all(f32[16,1,4096]{2,1,0:T(1,128)S(1)} %reshape.177), channel_id=1, replica_groups=mesh['gx'=16,'gy'=16] {'gx'}, dimensions={0} | all-to-all | bytes 524288 | tf_op jit(solution)/shard_map/all_to_all | solution.py:179
  379.1 2.6 copy.105
  381.7 2.8 all_to_all.255
  398.7 10.5 %all_to_all.297 = f32[16,1,4096]{2,1,0:T(1,128)S(1)} all-to-all(f32[16,1,4096]{2,1,0:T(1,128)S(1)} %reshape.179), channel_id=1, replica_groups=mesh['gx'=16,'gy'=16] {'gx'}, dimensions={0} | all-to-all | bytes 524288 | tf_op jit(solution)/shard_map/all_to_all | solution.py:158
  410.4 2.8 reshape.180
  413.2 1.9 copy.107
  416.6 1.7 copy.148
  420.9 1.8 copy.110
  423.5 13.9 %all_to_all.298 = f32[16,1,4096]{2,1,0:T(1,128)S(1)} all-to-all(f32[16,1,4096]{2,1,0:T(1,128)S(1)} %reshape.181), channel_id=1, replica_groups=mesh['gx'=16,'gy'=16] {'gy'}, dimensions={0} | all-to-all | bytes 524288 | tf_op jit(solution)/shard_map/all_to_all | solution.py:163
  439.3 2.0 copy.112
  441.3 2.7 all_to_all.263
  455.1 1.7 copy.113
  458.4 15.4 %all_to_all.299 = f32[16,1,4096]{2,1,0:T(1,128)S(1)} all-to-all(f32[16,1,4096]{2,1,0:T(1,128)S(1)} %reshape.183), channel_id=1, replica_groups=mesh['gx'=16,'gy'=16] {'gy'}, dimensions={0} | all-to-all | bytes 524288 | tf_op jit(solution)/shard_map/all_to_all | solution.py:175
  480.3 1.8 copy.117
  482.9 13.7 %all_to_all.300 = f32[16,1,4096]{2,1,0:T(1,128)S(1)} all-to-all(f32[16,1,4096]{2,1,0:T(1,128)S(1)} %reshape.185), channel_id=1, replica_groups=mesh['gx'=16,'gy'=16] {'gx'}, dimensions={0} | all-to-all | bytes 524288 | tf_op jit(solution)/shard_map/all_to_all | solution.py:179
  498.4 2.6 copy.119
  501.0 2.4 all_to_all.271
  (286 shorter events, 183.7 us)
Async XLA Ops:
  0.0 26.9 %copy-start.18 = (s32[2,16]{1,0:T(2,128)S(1)}, s32[2,16]{1,0:T(2,128)}, u32[]{:S(2)}) copy-start(s32[2,16]{1,0:T(2,128)} %param.13) | copy-start | bytes 388
  5.2 7.3 %collective-permute-start.1 = (f32[2,1,16,256]{3,0,2,1:T(2,128)S(1)}, f32[2,1,16,256]{3,0,2,1:T(2,128)S(1)}, u32[]{:S(2)}, u32[]{:S(2)}) collective-permute-start(f32[2,1,16,256]{3,0,2,1:T(2,128)S(1)} %get-tuple-element.46), channel_id=1, source_target_pairs={{0,16},{16,32},{32,48},{48,64},{64,80},{80,96},{96,112},{112,128},... | collective-permute-start | bytes 98312 | tf_op jit(solution)/shard_map/ppermute | solution.py:22
  7.9 4.7 collective-permute-start
  12.6 8.9 %collective-permute-start.2 = (f32[2,6,1,256]{3,0,2,1:T(2,128)S(1)}, f32[2,6,1,256]{3,0,2,1:T(2,128)S(1)}, u32[]{:S(2)}, u32[]{:S(2)}) collective-permute-start(f32[2,6,1,256]{3,0,2,1:T(2,128)S(1)} %get-tuple-element.40), channel_id=1, source_target_pairs={{1,0},{2,1},{3,2},{4,3},{5,4},{6,5},{7,6},{8,7},{9,8},{10,9},{11,1... | collective-permute-start | bytes 36872 | tf_op jit(solution)/shard_map/ppermute | solution.py:25
  20.1 6.2 %collective-permute-start.3 = (f32[2,6,1,256]{3,0,2,1:T(2,128)S(1)}, f32[2,6,1,256]{3,0,2,1:T(2,128)S(1)}, u32[]{:S(2)}, u32[]{:S(2)}) collective-permute-start(f32[2,6,1,256]{3,0,2,1:T(2,128)S(1)} %get-tuple-element.41), channel_id=1, source_target_pairs={{0,1},{1,2},{2,3},{3,4},{4,5},{5,6},{6,7},{7,8},{8,9},{9,10},{10,1... | collective-permute-start | bytes 36872 | tf_op jit(solution)/shard_map/ppermute | solution.py:22
  36.3 14.9 %all-to-all-start = ((f32[16,1,4096]{2,1,0:T(1,128)}), f32[16,1,4096]{2,1,0:T(1,128)S(1)}, u32[]{:S(2)}, u32[]{:S(2)}) async-start(f32[16,1,4096]{2,1,0:T(1,128)} %reshape.155), calls=%async_computation | async-start | bytes 524288 | tf_op jit(solution)/shard_map/all_to_all | solution.py:158
  59.1 2.7 copy-start
  66.7 13.8 %all-to-all-start.1 = ((f32[16,1,4096]{2,1,0:T(1,128)}), f32[16,1,4096]{2,1,0:T(1,128)S(1)}, u32[]{:S(2)}, u32[]{:S(2)}) async-start(f32[16,1,4096]{2,1,0:T(1,128)} %reshape.157), calls=%async_computation.1 | async-start | bytes 524288 | tf_op jit(solution)/shard_map/all_to_all | solution.py:163
  71.7 25.1 %copy-start.10 = (f32[4,256,16]{1,2,0:T(8,128)}, f32[4,256,16]{1,2,0:T(8,128)S(1)}, u32[]{:S(2)}) copy-start(f32[4,256,16]{1,2,0:T(8,128)S(1)} %get-tuple-element.52) | copy-start | bytes 196612
  71.7 25.1 %copy-start.14 = (f32[4,256,16]{1,2,0:T(8,128)}, f32[4,256,16]{1,2,0:T(8,128)S(1)}, u32[]{:S(2)}) copy-start(f32[4,256,16]{1,2,0:T(8,128)S(1)} %get-tuple-element.53) | copy-start | bytes 196612
  125.9 13.7 %all-to-all-start.3 = ((f32[16,1,4096]{2,1,0:T(1,128)}), f32[16,1,4096]{2,1,0:T(1,128)S(1)}, u32[]{:S(2)}, u32[]{:S(2)}) async-start(f32[16,1,4096]{2,1,0:T(1,128)} %reshape.161), calls=%async_computation.3 | async-start | bytes 524288 | tf_op jit(solution)/shard_map/all_to_all | solution.py:179
  132.5 19.8 %copy-start.4 = (f32[4,16,256]{2,1,0:T(8,128)}, f32[4,16,256]{2,1,0:T(8,128)S(1)}, u32[]{:S(2)}) copy-start(f32[4,16,256]{2,1,0:T(8,128)S(1)} %get-tuple-element.59) | copy-start | bytes 196612
  132.5 19.7 %copy-start.7 = (f32[4,16,256]{2,1,0:T(8,128)}, f32[4,16,256]{2,1,0:T(8,128)S(1)}, u32[]{:S(2)}) copy-start(f32[4,16,256]{2,1,0:T(8,128)S(1)} %get-tuple-element.60) | copy-start | bytes 196612
  178.8 2.7 copy-start.1
  206.5 5.5 %copy-start.11 = (f32[4,256,16]{1,2,0:T(8,128)S(1)}, f32[4,256,16]{1,2,0:T(8,128)}, u32[]{:S(2)}) copy-start(f32[4,256,16]{1,2,0:T(8,128)} %copy-done.10) | copy-start | bytes 196612
  206.5 5.5 %copy-start.15 = (f32[4,256,16]{1,2,0:T(8,128)S(1)}, f32[4,256,16]{1,2,0:T(8,128)}, u32[]{:S(2)}) copy-start(f32[4,256,16]{1,2,0:T(8,128)} %copy-done.14) | copy-start | bytes 196612
  268.5 2.9 copy-start.5
  268.5 2.9 copy-start.8
  298.1 2.7 copy-start.2
  325.0 5.5 %copy-start.12 = (f32[4,256,16]{1,2,0:T(8,128)S(1)}, f32[4,256,16]{1,2,0:T(8,128)}, u32[]{:S(2)}) copy-start(f32[4,256,16]{1,2,0:T(8,128)} %copy-done.10) | copy-start | bytes 196612
  325.0 5.5 %copy-start.16 = (f32[4,256,16]{1,2,0:T(8,128)S(1)}, f32[4,256,16]{1,2,0:T(8,128)}, u32[]{:S(2)}) copy-start(f32[4,256,16]{1,2,0:T(8,128)} %copy-done.14) | copy-start | bytes 196612
  388.6 1.6 copy-start.6
  388.6 1.6 copy-start.9
  416.6 2.7 copy-start.3
  444.0 5.5 %copy-start.13 = (f32[4,256,16]{1,2,0:T(8,128)S(1)}, f32[4,256,16]{1,2,0:T(8,128)}, u32[]{:S(2)}) copy-start(f32[4,256,16]{1,2,0:T(8,128)} %copy-done.10) | copy-start | bytes 196612
  444.0 5.5 %copy-start.17 = (f32[4,256,16]{1,2,0:T(8,128)S(1)}, f32[4,256,16]{1,2,0:T(8,128)}, u32[]{:S(2)}) copy-start(f32[4,256,16]{1,2,0:T(8,128)} %copy-done.14) | copy-start | bytes 196612
where the time goes:
time: 520 us; the launch traced here: 510 us
  blocking collectives  174 us (33%)
  local copies, waits for them, and re-layouts  140 us (27%)
  matrix products  104 us (20%)
  other arithmetic  29 us (6%)
  starting transfers between devices  28.7 us (6%)
  waiting for transfers between devices  28 us (5%)
  between operations  5.52 us (1%)
    all_to_all x4, blocking collectives, per_device(): lax.all_to_all(spectra, 'gy', split_axis=3, concat_axis=2, tiled=True)  60.8 us
    unnamed x88, local copies, waits for them, and re-layouts  55.6 us
    dot_general x32, matrix products, along(): return jnp.einsum('fxyz,ky->fxkz', values, matrix, precision=highest)  44 us
    dot_general x32, matrix products, along(): return jnp.einsum('fxyz,kz->fxyk', values, matrix, precision=highest)  43.1 us
    all_to_all x3, blocking collectives, per_device(): lax.all_to_all(spectra, 'gy', split_axis=2, concat_axis=3, tiled=True)  41.3 us
    all_to_all x3, blocking collectives, per_device(): lax.all_to_all(spectra, 'gx', split_axis=2, concat_axis=4, tiled=True)  40.7 us
    all_to_all x3, blocking collectives, per_device(): lax.all_to_all(spectra, 'gx', split_axis=4, concat_axis=2, tiled=True)  31.4 us
    all_to_all x8, local copies, waits for them, and re-layouts, per_device(): lax.all_to_all(spectra, 'gx', split_axis=2, concat_axis=4, tiled=True)  20.8 us
  transfers between devices with their start and end apart: 7, of which 4 were waited for; matrix products, arithmetic and copies ran while one was open for 1% of the time, Pallas kernels for 0%

commit v1 on v0

v1 whole, which is shorter than its diff:
```python
import functools
import math

import jax
import jax.numpy as jnp
import numpy as np
from jax import lax
from jax.experimental import pallas as pl
from jax.experimental.pallas import tpu as pltpu
from jax.sharding import PartitionSpec as P

ITERS = 4
GROUP = 16
MESH = pl.DeviceIdType.MESH
F32 = jnp.float32
BF16 = jnp.bfloat16
WAVE = 2.0 * math.pi / 6.0
GX_OUT, GY_OUT, GY_BACK, GX_BACK = range(4)


def transform_matrices():
    n = np.arange(128)
    phase = 2.0 * np.pi * (np.outer(n, n) % 128) / 128
    c, s = np.cos(phase), np.sin(phase)
    z_out = np.block([[c, s], [-s, c]])
    z_back = np.block([[c, -s], [s, c]])
    order = (np.arange(2)[None, :, None] * 128 + np.arange(16)[:, None, None] * 8 + np.arange(8)).reshape(-1)
    z_out = z_out[order]
    z_back = z_back[:, order]
    p, a, b = n >> 6, (n >> 4) & 3, n & 15
    phase = 2.0 * np.pi * ((4 * np.outer(a, a) + np.outer(b, b)) % 16) / 16
    same = p[:, None] == p[None, :]
    c, s = np.cos(phase) * same, np.sin(phase) * same
    xy_out = np.block([[c, -s], [s, c]])
    xy_back = np.block([[c, s], [-s, c]])
    parts = []
    for matrix in (z_out, z_back, xy_out, xy_back):
        high = matrix.astype(BF16)
        parts.append(high)
        parts.append((matrix - high.astype(np.float64)).astype(BF16))
    return np.stack(parts)


def cos_turn(m):
    m = m & 255
    t = (64 - jnp.minimum(m, 256 - m)).astype(F32) * (2.0 * math.pi / 256)
    q = t * t
    poly = -1.0 / 39916800
    for term in (1.0 / 362880, -1.0 / 5040, 1.0 / 120, -1.0 / 6, 1.0):
        poly = poly * q + term
    return t * poly


def backward_turn(m):
    return cos_turn(m), -cos_turn(m - 64)


def cmul(a, b):
    return a[0] * b[0] - a[1] * b[1], a[0] * b[1] + a[1] * b[0]


def cmul_conj(a, b):
    return a[0] * b[0] + a[1] * b[1], a[1] * b[0] - a[0] * b[1]


def box_sum(m):
    w = backward_turn(m)
    square = backward_turn(2 * m)
    return cmul((1.0 + w[0], w[1]), (1.0 + square[0], square[1]))


def dft4(a, sign):
    (r0, i0), (r1, i1), (r2, i2), (r3, i3) = a
    sr, si, dr, di = r0 + r2, i0 + i2, r0 - r2, i0 - i2
    tr, ti, ur, ui = r1 + r3, i1 + i3, r1 - r3, i1 - i3
    minus, plus = (dr + ui, di - ur), (dr - ui, di + ur)
    if sign > 0:
        minus, plus = plus, minus
    return [(sr + tr, si + ti), minus, (sr - tr, si - ti), plus]


def turn16(a, m, sign):
    if m == 0:
        return a
    r, i = a
    if m == 4:
        return (i, -r) if sign < 0 else (-i, r)
    c, s = math.cos(2 * math.pi * m / 16), sign * math.sin(2 * math.pi * m / 16)
    if m == 2 or m == 6:
        return _rot((r - i) * math.sqrt(0.5), (r + i) * math.sqrt(0.5), c, s)
    return r * c - i * s, r * s + i * c


def _rot(minus, plus, c, s):
    if c > 0 and s > 0:
        return minus, plus
    if c > 0:
        return plus, -minus
    if s > 0:
        return -plus, minus
    return -minus, -plus


def dft16(x, sign):
    inner = [dft4([x[4 * n1 + n2] for n1 in range(4)], sign) for n2 in range(4)]
    out = [None] * 16
    for k1 in range(4):
        column = [turn16(inner[n2][k1], n2 * k1, sign) for n2 in range(4)]
        for k2, value in enumerate(dft4(column, sign)):
            out[k1 + 4 * k2] = value
    return out


def split(x):
    high = x.astype(BF16)
    return high, (x - high.astype(F32)).astype(BF16)


def matmul(a, b):
    dot = functools.partial(jnp.dot, preferred_element_type=F32)
    return dot(a[0], b[0]) + (dot(a[0], b[1]) + dot(a[1], b[0]))


def lane_parts(lane):
    return lane >> 6, (lane >> 4) & 3, lane & 15


def swap_halves(t, sign):
    return pltpu.roll(t, 64, 1) + sign * t


def folded_square(index, length):
    wave = 2.0 * math.pi * jnp.where(index < length // 2, index, index - length).astype(F32) / length
    return wave * wave


def medium(speed, absorption):
    k = WAVE / speed
    real = k * k - absorption * absorption
    imag = 2.0 * k * absorption
    centre = 0.5 * (jnp.min(real, axis=1, keepdims=True) + jnp.max(real, axis=1, keepdims=True))
    size = jnp.sqrt((real - centre) ** 2 + imag * imag)
    return real, imag, centre, 1.05 * jnp.max(size, axis=1, keepdims=True)


def look_up(labels, table):
    out = jnp.broadcast_to(table[:, 0:1], labels.shape)
    for l in range(1, table.shape[1]):
        out = jnp.where(labels == l, table[:, l : l + 1], out)
    return out


def column(row):
    n = row.shape[1]
    eye = lax.broadcasted_iota(jnp.int32, (n, n), 0) == lax.broadcasted_iota(jnp.int32, (n, n), 1)
    spread_out = jnp.where(eye, jnp.broadcast_to(row.astype(F32), (n, n)), 0.0)
    return jnp.sum(spread_out, axis=1, keepdims=True)


def to_lanes(a):
    return jnp.concatenate([a[:, :128], a[:, 128:]], axis=0).T


def from_lanes(a):
    a = a.T
    return jnp.concatenate([a[:64], a[64:]], axis=1)


def smoothed(own, x_low, x_high, y_low, y_high):
    row = lax.broadcasted_iota(jnp.int32, own.shape, 0) & 15

    def per_x(edge):
        return jnp.concatenate([jnp.broadcast_to(edge[x : x + 1], (16, 256)) for x in range(4)], axis=0)

    total = jnp.concatenate([x_low, own[:48]], axis=0) + jnp.concatenate([own[16:], x_high], axis=0)
    total = total + jnp.where(row == 0, per_x(y_low), pltpu.roll(own, 1, 0))
    total = total + jnp.where(row == 15, per_x(y_high), pltpu.roll(own, 63, 0))
    total = total + pltpu.roll(own, 1, 1) + pltpu.roll(own, 255, 1)
    return 0.5 * own + total * (1.0 / 12.0)


def source_spectrum(amplitude, sx, sy, sz, gx, gy):
    lane = lax.broadcasted_iota(jnp.int32, (16, 128), 1)
    parity, x2, y2 = lane_parts(lane)
    row_phase = sy * (lane >> 3) + sz * (16 * gx + 2 * (lane & 7))
    pr, pi = backward_turn(row_phase)
    qr, qi = cmul(backward_turn(4 * sx * (gy + 16 * x2) + 16 * sy * y2 + sz * parity), amplitude)
    left = jnp.concatenate([pr, pi], axis=0)
    right = jnp.concatenate(
        [jnp.concatenate([qr, qi], axis=1), jnp.concatenate([-qi, qr], axis=1)], axis=0
    )
    return lax.dot_general(
        left.T, right, (((1,), (0,)), ((), ())), precision=lax.Precision.HIGHEST, preferred_element_type=F32
    )


def kernel(
    labels, speed, absorption, amplitude, source_x, source_y, source_z, matrix_hbm, out,
    matrix, send, recv, field, first, potential, turns, wturn, green, edge, near_x, near_y,
    matrix_sem, send_sem, recv_sem, edge_send, edge_recv,
):
    gx, gy = lax.axis_index("gx"), lax.axis_index("gy")

    load = pltpu.make_async_copy(matrix_hbm, matrix, matrix_sem)
    load.start()

    barrier = pltpu.get_barrier_semaphore()

    def greet(step, carry):
        pl.semaphore_signal(barrier, inc=1, device_id=(lax.rem(gx + step, GROUP), gy), device_id_type=MESH)
        pl.semaphore_signal(barrier, inc=1, device_id=(gx, lax.rem(gy + step, GROUP)), device_id_type=MESH)
        return carry

    lax.fori_loop(1, GROUP, greet, 0)

    def start(stage, f):
        along_x = stage in (GX_OUT, GX_BACK)
        me = gx if along_x else gy

        def one(step, carry):
            to = lax.rem(me + step, GROUP)
            pltpu.make_async_remote_copy(
                src_ref=send.at[stage, f, to],
                dst_ref=recv.at[stage, f, me],
                send_sem=send_sem.at[stage, f],
                recv_sem=recv_sem.at[stage, f],
                device_id=(to, gy) if along_x else (gx, to),
                device_id_type=MESH,
            ).start()
            return carry

        lax.fori_loop(1, GROUP, one, 0)
        recv[stage, f, me] = send[stage, f, me]

    def all_but_one(ref, stage, f, sem):
        part = ref.at[stage, f, pl.ds(0, GROUP - 1)]
        return pltpu.make_async_copy(part, part, sem.at[stage, f])

    def arrived(stage, f):
        all_but_one(recv, stage, f, recv_sem).wait()

    def sent(stage, f):
        all_but_one(send, stage, f, send_sem).wait()

    def blocks(stage, f):
        return [(recv[stage, f, g, 0:8], recv[stage, f, g, 8:16]) for g in range(GROUP)]

    def put(stage, f, values):
        for g, (real, imag) in enumerate(values):
            send[stage, f, g, 0:8] = real
            send[stage, f, g, 8:16] = imag

    def rows(values):
        return jnp.concatenate(
            [jnp.concatenate([v[0] for v in values], axis=0), jnp.concatenate([v[1] for v in values], axis=0)], axis=1
        )

    def unrows(values):
        return [(values[8 * g : 8 * g + 8, :128], values[8 * g : 8 * g + 8, 128:]) for g in range(GROUP)]

    def turn_row(g):
        return turns[0, g : g + 1], turns[1, g : g + 1]

    def y_back(f, spectrum):
        mixed = unrows(matmul(split(rows(spectrum)), (matrix[6], matrix[7])))
        put(GY_BACK, f, dft16([cmul_conj(v, turn_row(g)) for g, v in enumerate(mixed)], 1))
        start(GY_BACK, f)

    def y_both(f):
        values = dft16(blocks(GY_OUT, f), -1)
        values = [cmul(v, turn_row(g)) for g, v in enumerate(values)]
        mixed = unrows(matmul(split(rows(values)), (matrix[4], matrix[5])))
        y_back(f, [cmul(v, (green[0, g], green[1, g])) for g, v in enumerate(mixed)])

    def x_out(f):
        put(GY_OUT, f, dft16(blocks(GX_OUT, f), -1))
        start(GY_OUT, f)

    def x_back(f):
        put(GX_BACK, f, dft16(blocks(GY_BACK, f), 1))
        start(GX_BACK, f)

    lane = lax.broadcasted_iota(jnp.int32, (128, 128), 1)
    half = jnp.where(lane < 64, 1.0, -1.0).astype(F32)

    def z_out(f):
        v = cmul((potential[0], potential[1]), (field[f, 0], field[f, 1]))
        v = cmul((swap_halves(v[0], half), swap_halves(v[1], half)), (wturn[0], wturn[1]))
        values = matmul((matrix[0], matrix[1]), split(jnp.concatenate(v, axis=0)))
        send[GX_OUT, f] = values.reshape(GROUP, 16, 128)
        start(GX_OUT, f)

    def z_back(f):
        values = matmul((matrix[2], matrix[3]), split(recv[GX_BACK, f].reshape(256, 128)))
        v = cmul_conj((values[:128], values[128:]), (wturn[0], wturn[1]))
        return swap_halves(v[0], half), swap_halves(v[1], half)

    def change_of(c, inverse):
        w = cmul((potential[0], potential[1]), c)
        return -w[1] * inverse, w[0] * inverse

    table_real, table_imag, centre, spread = medium(speed[...], absorption[...])
    inverse = 1.0 / spread

    lane16 = lax.broadcasted_iota(jnp.int32, (16, 128), 1)
    row16 = lax.broadcasted_iota(jnp.int32, (16, 128), 0)
    _, x16, y16 = lane_parts(lane16)
    turns[0], turns[1] = backward_turn(y16 * row16 + 4 * x16 * gy)
    lane8 = lax.broadcasted_iota(jnp.int32, (8, 128), 1)
    row8 = lax.broadcasted_iota(jnp.int32, (8, 128), 0)
    parity, x2, y2 = lane_parts(lane8)
    kx = gy + 16 * x2
    kz = 2 * (8 * gx + row8) + parity
    ky = row16 + 16 * y16
    beside = folded_square(kx, 64) + folded_square(kz, 256)
    wave_y = folded_square(ky, 256)
    box_xz = cmul(box_sum(4 * kx), box_sum(kz))
    box_y = box_sum(ky)
    scale = 1.0 / (64 * 256 * 256)
    weights = []
    for g in range(GROUP):
        shifted = (beside + wave_y[g : g + 1]) - centre
        share = scale / (shifted * shifted + spread * spread)
        value = (shifted * share, spread * share)
        green[0, g], green[1, g] = value
        weights.append(cmul(cmul(value, (box_y[0][g : g + 1], box_y[1][g : g + 1])), box_xz))
    load.wait()

    for x in range(4):
        edge[x : x + 1] = labels[x, 0:1]
        edge[4 + x : 5 + x] = labels[x, 15:16]

    spectra = []
    for f in range(2):
        amp = (amplitude[f, :, 0:1], amplitude[f, :, 1:2])
        corner = [column(s[f : f + 1]).astype(jnp.int32) for s in (source_x, source_y, source_z)]
        spectrum = unrows(source_spectrum(amp, *corner, gx, gy))
        spectra.append([cmul(v, w) for v, w in zip(spectrum, weights)])

    pl.semaphore_wait(barrier, 2 * (GROUP - 1))
    for f in range(2):
        y_back(f, spectra[f])

    up_x, down_x = lax.rem(gx + 1, GROUP), lax.rem(gx + GROUP - 1, GROUP)
    up_y, down_y = lax.rem(gy + 1, GROUP), lax.rem(gy + GROUP - 1, GROUP)
    edges = [
        pltpu.make_async_remote_copy(
            src_ref=source, dst_ref=target, send_sem=edge_send.at[k], recv_sem=edge_recv.at[k],
            device_id=device, device_id_type=MESH,
        )
        for k, (source, target, device) in enumerate(
            (
                (labels.at[3], near_x.at[0], (up_x, gy)),
                (labels.at[0], near_x.at[1], (down_x, gy)),
                (edge, near_y.at[0], (gx, up_y)),
                (edge, near_y.at[1], (gx, down_y)),
            )
        )
    ]
    for copy in edges:
        copy.start()

    z_low = lax.broadcasted_iota(jnp.int32, (128, 128), 0)
    wturn[0], wturn[1] = backward_turn(jnp.where(lane < 64, 0, z_low))
    for copy in edges:
        copy.wait()
    own = labels[...].reshape(64, 256)
    for part, (table, shift) in enumerate(((table_real, centre), (table_imag, spread))):
        values = [look_up(a, table) for a in (own, near_x[0], near_x[1], near_y[0, 4:8], near_y[1, 0:4])]
        potential[part] = to_lanes(smoothed(*values) - shift)

    for f in range(2):
        arrived(GY_BACK, f)
        x_back(f)
    for f in range(2):
        arrived(GX_BACK, f)
        v = z_back(f)
        first[f, 0], first[f, 1] = v
        field[f, 0], field[f, 1] = change_of(v, inverse)
        z_out(f)

    def iteration(step, carry):
        for f in range(2):
            arrived(GX_OUT, f)

            @pl.when(step > 0)
            def _():
                sent(GY_OUT, f)

            x_out(f)
        for f in range(2):
            arrived(GY_OUT, f)
            sent(GY_BACK, f)
            y_both(f)
        for f in range(2):
            arrived(GY_BACK, f)
            sent(GX_BACK, f)
            x_back(f)
        for f in range(2):
            arrived(GX_BACK, f)
            v = z_back(f)
            real, imag = field[f, 0], field[f, 1]
            move = change_of((v[0] + first[f, 0] - real, v[1] + first[f, 1] - imag), inverse)
            field[f, 0], field[f, 1] = real + move[0], imag + move[1]

            @pl.when(step < ITERS - 2)
            def _():
                sent(GX_OUT, f)
                z_out(f)

        return carry

    lax.fori_loop(0, ITERS - 1, iteration, 0)

    for f in range(2):
        for part in range(2):
            out[f, part] = from_lanes(field[f, part]).reshape(4, 16, 256)
    for stage in range(4):
        for f in range(2):
            sent(stage, f)


def per_device(labels, speed, absorption, amplitude, source_x, source_y, source_z):
    vmem = pl.BlockSpec(memory_space=pltpu.VMEM)
    return pl.pallas_call(
        kernel,
        out_shape=jax.ShapeDtypeStruct((2, 2, 4, 16, 256), F32),
        in_specs=[vmem] * 7 + [pl.BlockSpec(memory_space=pl.ANY)],
        out_specs=vmem,
        scratch_shapes=[
            pltpu.VMEM((8, 256, 256), BF16),
            pltpu.VMEM((4, 2, GROUP, 16, 128), F32),
            pltpu.VMEM((4, 2, GROUP, 16, 128), F32),
            pltpu.VMEM((2, 2, 128, 128), F32),
            pltpu.VMEM((2, 2, 128, 128), F32),
            pltpu.VMEM((2, 128, 128), F32),
            pltpu.VMEM((2, 16, 128), F32),
            pltpu.VMEM((2, 128, 128), F32),
            pltpu.VMEM((2, GROUP, 8, 128), F32),
            pltpu.VMEM((8, 256), jnp.int32),
            pltpu.VMEM((2, 16, 256), jnp.int32),
            pltpu.VMEM((2, 8, 256), jnp.int32),
            pltpu.SemaphoreType.DMA,
            pltpu.SemaphoreType.DMA((4, 2)),
            pltpu.SemaphoreType.DMA((4, 2)),
            pltpu.SemaphoreType.DMA((4,)),
            pltpu.SemaphoreType.DMA((4,)),
        ],
        compiler_params=pltpu.CompilerParams(
            collective_id=0, has_side_effects=True, vmem_limit_bytes=32 * 1024 * 1024
        ),
    )(
        labels,
        speed.reshape(1, 8),
        absorption.reshape(1, 8),
        amplitude,
        source_x,
        source_y,
        source_z,
        jnp.asarray(transform_matrices()),
    )


def solution(mesh):
    return jax.shard_map(
        per_device,
        mesh=mesh,
        in_specs=(P("gx", "gy", None), P(), P(), P(), P(), P(), P()),
        out_specs=P(None, None, "gx", "gy", None),
        check_vma=False,
    )
```

time: 520 us -> 110 us (0.21); the launches traced: 510 us -> 110 us
  blocking collectives: 174 us -> 0 us
  local copies, waits for them, and re-layouts: 140 us -> 4.15 us
  Pallas kernels: 0 us -> 105 us
  matrix products: 104 us -> 0 us
  other arithmetic: 29 us -> 0 us
  starting transfers between devices: 28.7 us -> 0 us
  waiting for transfers between devices: 28 us -> 0 us
  between operations: 5.52 us -> 0.03 us
    all_to_all x13 -> x0, blocking collectives: 174 us -> none  [the longest x4 60.8 us: per_device(): lax.all_to_all(spectra, 'gy', split_axis=3, concat_axis=2, tiled=True)]
    pallas_call x0 -> x1, Pallas kernels: none -> 105 us  [per_device(): pl.pallas_call(kernel, out_shape=jax.ShapeDtypeStruct((2, 2, 4, 16, 256),...]
    dot_general x66 -> x0, matrix products: 88.6 us -> none  [the longest x32 44 us: along(): return jnp.einsum('fxyz,ky->fxkz', values, matrix, precision=highest)]
    unnamed x88 -> x18, local copies, waits for them, and re-layouts: 55.6 us -> 4.15 us
    all_to_all x25 -> x0, local copies, waits for them, and re-layouts: 50.7 us -> none  [the longest x8 20.8 us: per_device(): lax.all_to_all(spectra, 'gx', split_axis=2, concat_axis=4, tiled=True)]
    another operation x17 -> x0, local copies, waits for them, and re-layouts: 26.8 us -> none  [the longest x8 13.6 us: transform(): return jnp.stack([cos_real - sin_imag, cos_imag + sin_real], axis=1)]
    all_to_all x3 -> x0, waiting for transfers between devices: 23.1 us -> none  [the longest x1 8.79 us: per_device(): lax.all_to_all(spectra, 'gy', split_axis=2, concat_axis=3, tiled=True)]
    all_to_all x16 -> x0, other arithmetic: 18.8 us -> none  [the longest x4 4.69 us: per_device(): lax.all_to_all(spectra, 'gy', split_axis=2, concat_axis=3, tiled=True)]
  transfers between devices with their start and end apart: 7 -> 0, of which waited for: 4 -> 0; matrix products, arithmetic and copies ran while one was open for 1% -> 0% of each run, Pallas kernels for 0% -> 0%
where the time goes in v1:
time: 110 us
  Pallas kernels  105 us (95%)
  local copies, waits for them, and re-layouts  4.15 us (4%)
    pallas_call x1, Pallas kernels, per_device(): pl.pallas_call(kernel, out_shape=jax.ShapeDtypeStruct((2, 2, 4, 16, 256),...  105 us
    unnamed x18, local copies, waits for them, and re-layouts  4.15 us

profile of v1, /device:TPU:1, one launch (start us, length us, event | category | flops | bytes accessed | tf_op | source)
XLA Modules:
  0.0 109.5 jit_solution(2151364450438883445)
XLA Ops:
  0.0 0.0 copy-start.7
  0.0 0.7 copy-done.7
  0.7 0.0 copy-start.2
  0.7 0.0 copy-start.3
  0.7 0.0 copy-start.4
  0.7 0.0 copy-start.5
  0.7 0.0 copy-start.6
  0.7 0.1 copy.9.amplitude
  0.8 0.6 copy-done.2
  1.4 0.0 copy-done.3
  1.4 0.0 copy-done.4
  1.4 0.0 copy-done.5
  1.4 0.0 copy-done.6
  1.4 0.0 copy-start
  1.4 1.2 %copy-done = bf16[8,256,256]{2,1,0:T(8,128)(2,1)S(1)} copy-done((bf16[8,256,256]{2,1,0:T(8,128)(2,1)S(1)}, bf16[8,256,256]{2,1,0:T(8,128)(2,1)}, u32[]{:S(2)}) %copy-start) | copy-done | bytes 1048600
  2.6 0.0 copy-start.1
  2.6 0.8 copy-done.1
  3.5 105.3 %shard_map.82 = f32[2,2,4,16,256]{4,3,2,1,0:T(8,128)S(1)} custom-call(s32[4,16,256]{2,1,0:T(8,128)S(1)} %copy-done.1, f32[1,8]{1,0:T(1,128)S(1)} %bitcast.2, f32[1,8]{1,0:T(1,128)S(1)} %bitcast.3, f32[2,16,2]{2,1,0:T(8,128)S(1)} %copy.9.amplitude, s32[2,16]{1,0:T(2,128)S(1)} %copy-done.2, s32[2,16]{1,0:T(2,128)S(1)} %copy-done.3, s32[2,16]{1,0:T(2,128)S(1)} %copy-done.4, ...), custom_call_target="tpu_custom_call" | custom-call | tf_op jit(solution)/shard_map/pallas_call | solution.py:425
  108.8 0.7 copy.11
Async XLA Ops:
  0.0 0.7 copy-start.7
  0.7 0.7 copy-start.2
  0.7 0.7 copy-start.3
  0.7 0.7 copy-start.4
  0.7 0.7 copy-start.5
  0.7 0.7 copy-start.6
  1.4 1.2 %copy-start = (bf16[8,256,256]{2,1,0:T(8,128)(2,1)S(1)}, bf16[8,256,256]{2,1,0:T(8,128)(2,1)}, u32[]{:S(2)}) copy-start(bf16[8,256,256]{2,1,0:T(8,128)(2,1)} %constant.2.clone.matrix_hbm) | copy-start | bytes 3145732
  2.6 0.8 copy-start.1

commit v2 on v0

v2 whole, which is shorter than its diff:
```python
import functools
import math

import jax
import jax.numpy as jnp
import numpy as np
from jax import lax
from jax.experimental import pallas as pl
from jax.experimental.pallas import tpu as pltpu
from jax.sharding import PartitionSpec as P

ITERS = 4
CHIPS = 128
MESH = pl.DeviceIdType.MESH
F32 = jnp.float32
BF16 = jnp.bfloat16
WAVE = 2.0 * math.pi / 6.0
OUT, BACK = range(2)


def transform_matrices():
    def both(phase):
        c, s = np.cos(2.0 * np.pi * phase), np.sin(2.0 * np.pi * phase)
        return np.block([[c, s], [-s, c]]), np.block([[c, -s], [s, c]])

    n = np.arange(128)
    pairs = (np.arange(2)[None, :] * 128 + n[:, None]).reshape(-1)
    z_out, z_back = both((np.outer(n, n) % 128) / 128)
    high, low = n >> 4, n & 15
    mixed = ((2 * np.outer(high, high) + np.outer(low, low)) % 16) / 16
    far_out, far_back = both(mixed)
    near_back, near_out = both(mixed)
    parts = []
    for matrix in (z_out[pairs], z_back[:, pairs], far_out[:, pairs], far_back[pairs], near_out, near_back):
        high = matrix.astype(BF16)
        parts.append(high)
        parts.append((matrix - high.astype(np.float64)).astype(BF16))
    return np.stack(parts)


def constant_tables():
    n = np.arange(128)
    row, lane = n[:, None], n[None, :]
    z_turn = np.exp(-2j * np.pi * row / 256) * np.ones((1, 128))
    xy_turn = np.exp(-2j * np.pi * ((row >> 4) * (lane >> 4) / 64 + (row & 15) * (lane & 15) / 256))
    kx, ky = (row >> 4) + 8 * (lane >> 4), (row & 15) + 16 * (lane & 15)
    box = sum(np.exp(-2j * np.pi * j * kx / 64) for j in range(4)) * sum(np.exp(-2j * np.pi * j * ky / 256) for j in range(4))
    wave = [
        (2.0 * np.pi * np.where(k < size // 2, k, k - size) / size).astype(np.float32) for k, size in ((kx, 64), (ky, 256))
    ]
    tables = [z_turn.real, z_turn.imag, xy_turn.real, xy_turn.imag, box.real, box.imag]
    return np.stack([t.astype(np.float32) for t in tables] + [wave[0] * wave[0] + wave[1] * wave[1]])


def cos_turn(m):
    m = m & 255
    t = (64 - jnp.minimum(m, 256 - m)).astype(F32) * (2.0 * math.pi / 256)
    q = t * t
    poly = -1.0 / 39916800
    for term in (1.0 / 362880, -1.0 / 5040, 1.0 / 120, -1.0 / 6, 1.0):
        poly = poly * q + term
    return t * poly


def backward_turn(m):
    return cos_turn(m), -cos_turn(m - 64)


def cmul(a, b):
    return a[0] * b[0] - a[1] * b[1], a[0] * b[1] + a[1] * b[0]


def cmul_conj(a, b):
    return a[0] * b[0] + a[1] * b[1], a[1] * b[0] - a[0] * b[1]


def box_sum(m):
    w = backward_turn(m)
    square = backward_turn(2 * m)
    return cmul((1.0 + w[0], w[1]), (1.0 + square[0], square[1]))


def split(x):
    high = x.astype(BF16)
    return high, (x - high.astype(F32)).astype(BF16)


def matmul(a, b):
    dot = functools.partial(jnp.dot, preferred_element_type=F32)
    return dot(a[0], b[0]) + (dot(a[0], b[1]) + dot(a[1], b[0]))


def medium(speed, absorption):
    k = WAVE / speed
    real = k * k - absorption * absorption
    imag = 2.0 * k * absorption
    centre = 0.5 * (jnp.min(real, axis=1, keepdims=True) + jnp.max(real, axis=1, keepdims=True))
    size = jnp.sqrt((real - centre) ** 2 + imag * imag)
    return real, imag, centre, 1.05 * jnp.max(size, axis=1, keepdims=True)


def look_up(labels, table):
    out = jnp.broadcast_to(table[:, 0:1], labels.shape)
    for l in range(1, table.shape[1]):
        out = jnp.where(labels == l, table[:, l : l + 1], out)
    return out


def column(row):
    n = row.shape[1]
    eye = lax.broadcasted_iota(jnp.int32, (n, n), 0) == lax.broadcasted_iota(jnp.int32, (n, n), 1)
    spread_out = jnp.where(eye, jnp.broadcast_to(row.astype(F32), (n, n)), 0.0)
    return jnp.sum(spread_out, axis=1, keepdims=True)


def smoothed(own, x_low, x_high, y_low, y_high):
    row = lax.broadcasted_iota(jnp.int32, own.shape, 0) & 15

    def per_x(edge):
        return jnp.concatenate([jnp.broadcast_to(edge[x : x + 1], (16, 256)) for x in range(8)], axis=0)

    total = jnp.concatenate([x_low, own[:112]], axis=0) + jnp.concatenate([own[16:], x_high], axis=0)
    total = total + jnp.where(row == 0, per_x(y_low), pltpu.roll(own, 1, 0))
    total = total + jnp.where(row == 15, per_x(y_high), pltpu.roll(own, 127, 0))
    total = total + pltpu.roll(own, 1, 1) + pltpu.roll(own, 255, 1)
    return 0.5 * own + total * (1.0 / 12.0)


def farthest_first():
    offsets = [(y, x, z) for y in range(4) for x in range(4) for z in range(8)][1:]
    return sorted(offsets, key=lambda o: -(min(o[0], 4 - o[0]) + min(o[1], 4 - o[1]) + min(o[2], 8 - o[2])))


def kernel(
    labels_hbm, speed_hbm, absorption_hbm, amplitude_hbm, sx_hbm, sy_hbm, sz_hbm, matrix_hbm, table_hbm, out,
    speed, absorption, amplitude, sx, sy, sz, matrix, table,
    labels, near_x, near_y, edge, potential, field, first, green, spectrum, result, send, recv,
    load_sem, send_sem, recv_sem, edge_send, edge_recv, half_send, half_recv,
):
    gx, gy = lax.axis_index("gx"), lax.axis_index("gy")
    core, chip_x = lax.rem(gx, 2), gx // 2
    me = chip_x * 16 + gy
    sibling = chip_x * 2 + 1 - core
    next_x, last_x = lax.rem(chip_x + 1, 8), lax.rem(chip_x + 7, 8)
    next_y, last_y = lax.rem(gy + 1, 16), lax.rem(gy + 15, 16)

    loads = [
        pltpu.make_async_copy(source, target, load_sem.at[k])
        for k, (source, target) in enumerate(
            (
                (labels_hbm, labels.at[pl.ds(4 * core, 4)]),
                (speed_hbm, speed),
                (absorption_hbm, absorption),
                (amplitude_hbm, amplitude),
                (sx_hbm, sx),
                (sy_hbm, sy),
                (sz_hbm, sz),
                (table_hbm, table),
                (matrix_hbm, matrix),
            )
        )
    ]
    for load in loads:
        load.start()

    place_y, place_x, place_z = 2 * (gy // 8) + gx // 8, lax.rem(chip_x, 4), lax.rem(gy, 8)
    ys = [lax.rem(place_y + d, 4) for d in range(4)]
    xs = [lax.rem(place_x + d, 4) for d in range(4)]
    zs = [lax.rem(place_z + d, 8) for d in range(8)]
    to_x = [[lax.rem(y, 2) * 4 + x for x in xs] for y in ys]
    to_y = [[(y // 2) * 8 + z for z in zs] for y in ys]
    order = farthest_first()

    barrier = pltpu.get_barrier_semaphore()

    def greet(device):
        pl.semaphore_signal(barrier, inc=1, device_id=device, device_id_type=MESH)

    for y, x, z in order:
        greet((2 * to_x[y][x] + core, to_y[y][z]))
    greet((sibling, gy))
    greet((2 * next_x + 1 - core, gy))
    greet((2 * last_x + 1 - core, gy))
    greet((sibling, next_y))
    greet((sibling, last_y))

    def start(stage, p):
        target = recv.at[stage, p, pl.ds(2 * me, 2)]
        for y, x, z in order:
            pltpu.make_async_remote_copy(
                src_ref=send.at[stage, p, pl.ds(2 * (to_x[y][x] * 16 + to_y[y][z]), 2)],
                dst_ref=target,
                send_sem=send_sem.at[stage, p],
                recv_sem=recv_sem.at[stage, p],
                device_id=(2 * to_x[y][x] + core, to_y[y][z]),
                device_id_type=MESH,
            ).start()
        pltpu.make_async_copy(send.at[stage, p, pl.ds(2 * me, 2)], target, recv_sem.at[stage, p]).start()

    def arrived(stage, p):
        whole = recv.at[stage, p]
        pltpu.make_async_copy(whole, whole, recv_sem.at[stage, p]).wait()

    def sent(stage, p):
        part = send.at[stage, p, pl.ds(0, 2 * CHIPS - 2)]
        pltpu.make_async_copy(part, part, send_sem.at[stage, p]).wait()

    def weights(k):
        return matrix[2 * k], matrix[2 * k + 1]

    def turns(k):
        return table[2 * k], table[2 * k + 1]

    def halves(a):
        return a[:128], a[128:]

    def sides(a):
        return a[:, :128], a[:, 128:]

    def beside(v):
        return jnp.concatenate(v, axis=1)

    def below(v):
        return jnp.concatenate(v, axis=0)

    for load in loads[1:8]:
        load.wait()
    table_real, table_imag, centre, spread = medium(speed[...], absorption[...])
    inverse = 1.0 / spread

    def pick(ref):
        return column(jnp.where(core == 0, ref[0:1], ref[1:2]))

    corner_x, corner_y, corner_z = [pick(ref).astype(jnp.int32) for ref in (sx, sy, sz)]
    strength = tuple(column(jnp.where(core == 0, amplitude[0, k : k + 1], amplitude[1, k : k + 1])) for k in range(2))
    lane = lax.broadcasted_iota(jnp.int32, (16, 128), 1)
    high, low = lane >> 4, lane & 15
    left = below(backward_turn(4 * corner_x * high + corner_y * low)).T
    for p in range(2):
        kz = 2 * me + p
        folded = jnp.where(kz < 128, kz, kz - 256).astype(F32)
        wave_z = 2.0 * math.pi * jnp.full((1, 1), folded, F32) / 256
        shifted = (table[6] + wave_z * wave_z) - centre
        share = (1.0 / (64 * 256 * 256)) / (shifted * shifted + spread * spread)
        value = (shifted * share, spread * share)
        green[p, 0], green[p, 1] = value
        amount = cmul(strength, box_sum(jnp.full((16, 1), kz, jnp.int32)))
        q = cmul(backward_turn(32 * corner_x * high + 16 * corner_y * low + corner_z * kz), amount)
        right = below((beside(q), beside((-q[1], q[0]))))
        sums = jnp.dot(left, right, precision=lax.Precision.HIGHEST, preferred_element_type=F32)
        spectrum[p] = beside(cmul(sides(sums), cmul(value, turns(2))))
    field[...] = jnp.zeros_like(field)
    first[...] = jnp.zeros_like(first)
    loads[0].wait()
    loads[8].wait()
    for x in range(4):
        edge[x : x + 1] = labels[4 * core + x, 0:1]
        edge[4 + x : 5 + x] = labels[4 * core + x, 15:16]
    pl.semaphore_wait(barrier, CHIPS - 1 + 5)

    def to_others(k, source, target, recv_index, device):
        return pltpu.make_async_remote_copy(
            src_ref=source, dst_ref=target, send_sem=edge_send.at[k], recv_sem=edge_recv.at[recv_index],
            device_id=device, device_id_type=MESH,
        )

    def medium_of_cells():
        own = labels.at[pl.ds(4 * core, 4)]
        beside_x = lax.rem(chip_x + 7 + 2 * core, 8)
        copies = [to_others(0, own, own, 0, (sibling, gy))]
        for c in range(2):
            copies.append(
                to_others(1 + c, labels.at[7 * core], near_x.at[1 - core], 2 - core, (2 * beside_x + c, gy))
            )
            for d, to in enumerate((next_y, last_y)):
                copies.append(
                    to_others(3 + 2 * d + c, edge, near_y.at[d, core], 3 + 2 * d + core, (2 * chip_x + c, to))
                )
        for copy in copies:
            copy.start()
        theirs = labels.at[pl.ds(4 - 4 * core, 4)]
        landed = [theirs, near_x.at[0], near_x.at[1]] + [near_y.at[d, c] for d in range(2) for c in range(2)]
        for k, ref in enumerate(landed):
            pltpu.make_async_copy(ref, ref, edge_recv.at[k]).wait()
        for copy in copies:
            copy.wait_send()
        all_labels = labels[...].reshape(128, 256)
        y_low = below((near_y[0, 0, 4:8], near_y[0, 1, 4:8]))
        y_high = below((near_y[1, 0, 0:4], near_y[1, 1, 0:4]))
        for part, (entries, shift) in enumerate(((table_real, centre), (table_imag, spread))):
            values = [look_up(a, entries) for a in (all_labels, near_x[0], near_x[1], y_low, y_high)]
            moved = smoothed(*values) - shift
            potential[part, 0:128] = moved[:, :128].T
            potential[part, 128:256] = moved[:, 128:].T

    def iteration(step, carry):
        for p in range(2):

            @pl.when(step > 0)
            def _():
                arrived(OUT, p)
                v = cmul(halves(matmul(weights(2), split(recv[OUT, p]))), turns(1))
                v = sides(matmul(split(beside(v)), weights(4)))
                spectrum[p] = beside(cmul(v, (green[p, 0], green[p, 1])))
                sent(BACK, p)

            v = cmul_conj(sides(matmul(split(spectrum[p]), weights(5))), turns(1))
            send[BACK, p] = matmul(weights(3), split(below(v)))
            start(BACK, p)

        @pl.when(step == 0)
        def _():
            medium_of_cells()

        arrived(BACK, 0)
        even = halves(matmul(weights(1), split(recv[BACK, 0])))
        arrived(BACK, 1)
        odd = cmul_conj(halves(matmul(weights(1), split(recv[BACK, 1]))), turns(0))
        scattered = [below((even[k] + odd[k], even[k] - odd[k])) for k in range(2)]
        change = [scattered[k] + first[k] - field[k] for k in range(2)]
        moved = cmul((potential[0], potential[1]), change)
        field[0], field[1] = field[0] - moved[1] * inverse, field[1] + moved[0] * inverse

        @pl.when(step == 0)
        def _():
            first[0], first[1] = scattered

        @pl.when(step < ITERS - 1)
        def _():
            v = cmul((potential[0], potential[1]), (field[0], field[1]))
            upper, lower = halves(v[0]), halves(v[1])
            inputs = (
                (upper[0] + upper[1], lower[0] + lower[1]),
                cmul((upper[0] - upper[1], lower[0] - lower[1]), turns(0)),
            )
            for p in range(2):

                @pl.when(step > 0)
                def _():
                    sent(OUT, p)

                send[OUT, p] = matmul(weights(0), split(below(inputs[p])))
                start(OUT, p)

        return carry

    lax.fori_loop(0, ITERS, iteration, 0)

    for part in range(2):
        result[part] = beside((field[part, 0:128].T, field[part, 128:256].T)).reshape(8, 16, 256)
    theirs = pltpu.make_async_remote_copy(
        src_ref=result.at[:, pl.ds(4 - 4 * core, 4)], dst_ref=out.at[core], send_sem=half_send, recv_sem=half_recv,
        device_id=(sibling, gy), device_id_type=MESH,
    )
    theirs.start()
    out[core] = result[:, pl.ds(4 * core, 4)]
    landed = out.at[1 - core]
    pltpu.make_async_copy(landed, landed, half_recv).wait()
    theirs.wait_send()
    for stage in range(2):
        for p in range(2):
            sent(stage, p)


def per_device(labels, speed, absorption, amplitude, source_x, source_y, source_z):
    anywhere = pl.BlockSpec(memory_space=pl.ANY)
    dma = pltpu.SemaphoreType.DMA
    return pl.pallas_call(
        kernel,
        out_shape=jax.ShapeDtypeStruct((2, 2, 4, 16, 256), F32),
        in_specs=[anywhere] * 9,
        out_specs=pl.BlockSpec(memory_space=pltpu.VMEM),
        scratch_shapes=[
            pltpu.VMEM((1, 8), F32),
            pltpu.VMEM((1, 8), F32),
            pltpu.VMEM((2, 2, 16), F32),
            pltpu.VMEM((2, 16), jnp.int32),
            pltpu.VMEM((2, 16), jnp.int32),
            pltpu.VMEM((2, 16), jnp.int32),
            pltpu.VMEM((12, 256, 256), BF16),
            pltpu.VMEM((7, 128, 128), F32),
            pltpu.VMEM((8, 16, 256), jnp.int32),
            pltpu.VMEM((2, 16, 256), jnp.int32),
            pltpu.VMEM((2, 2, 8, 256), jnp.int32),
            pltpu.VMEM((8, 256), jnp.int32),
            pltpu.VMEM((2, 256, 128), F32),
            pltpu.VMEM((2, 256, 128), F32),
            pltpu.VMEM((2, 256, 128), F32),
            pltpu.VMEM((2, 2, 128, 128), F32),
            pltpu.VMEM((2, 128, 256), F32),
            pltpu.VMEM((2, 8, 16, 256), F32),
            pltpu.VMEM((2, 2, 2 * CHIPS, 128), F32),
            pltpu.VMEM((2, 2, 2 * CHIPS, 128), F32),
            dma((9,)),
            dma((2, 2)),
            dma((2, 2)),
            dma((7,)),
            dma((7,)),
            dma,
            dma,
        ],
        compiler_params=pltpu.CompilerParams(
            collective_id=0, has_side_effects=True, vmem_limit_bytes=56 * 1024 * 1024
        ),
    )(
        labels,
        speed.reshape(1, 8),
        absorption.reshape(1, 8),
        jnp.transpose(amplitude, (0, 2, 1)),
        source_x,
        source_y,
        source_z,
        jnp.asarray(transform_matrices()),
        jnp.asarray(constant_tables()),
    )


def solution(mesh):
    return jax.shard_map(
        per_device,
        mesh=mesh,
        in_specs=(P("gx", "gy", None), P(), P(), P(), P(), P(), P()),
        out_specs=P(None, None, "gx", "gy", None),
        check_vma=False,
    )
```

time: 520 us -> 82.9 us (0.16); the launches traced: 510 us -> 82.7 us
  blocking collectives: 174 us -> 0 us
  local copies, waits for them, and re-layouts: 140 us -> 1.67 us
  matrix products: 104 us -> 0 us
  Pallas kernels: 0 us -> 81.1 us
  other arithmetic: 29 us -> 0 us
  starting transfers between devices: 28.7 us -> 0 us
  waiting for transfers between devices: 28 us -> 0 us
  between operations: 5.52 us -> 0.01 us
    all_to_all x13 -> x0, blocking collectives: 174 us -> none  [the longest x4 60.8 us: per_device(): lax.all_to_all(spectra, 'gy', split_axis=3, concat_axis=2, tiled=True)]
    dot_general x66 -> x0, matrix products: 88.6 us -> none  [the longest x32 44 us: along(): return jnp.einsum('fxyz,ky->fxkz', values, matrix, precision=highest)]
    pallas_call x0 -> x1, Pallas kernels: none -> 81.1 us  [per_device(): pl.pallas_call(kernel, out_shape=jax.ShapeDtypeStruct((2, 2, 4, 16, 256),...]
    unnamed x88 -> x1, local copies, waits for them, and re-layouts: 55.6 us -> 1.67 us
    all_to_all x25 -> x0, local copies, waits for them, and re-layouts: 50.7 us -> none  [the longest x8 20.8 us: per_device(): lax.all_to_all(spectra, 'gx', split_axis=2, concat_axis=4, tiled=True)]
    another operation x17 -> x0, local copies, waits for them, and re-layouts: 26.8 us -> none  [the longest x8 13.6 us: transform(): return jnp.stack([cos_real - sin_imag, cos_imag + sin_real], axis=1)]
    all_to_all x3 -> x0, waiting for transfers between devices: 23.1 us -> none  [the longest x1 8.79 us: per_device(): lax.all_to_all(spectra, 'gy', split_axis=2, concat_axis=3, tiled=True)]
    all_to_all x16 -> x0, other arithmetic: 18.8 us -> none  [the longest x4 4.69 us: per_device(): lax.all_to_all(spectra, 'gy', split_axis=2, concat_axis=3, tiled=True)]
  transfers between devices with their start and end apart: 7 -> 0, of which waited for: 4 -> 0; matrix products, arithmetic and copies ran while one was open for 1% -> 0% of each run, Pallas kernels for 0% -> 0%
where the time goes in v2:
time: 82.9 us; the launch traced here: 82.7 us
  Pallas kernels  81.1 us (98%)
  local copies, waits for them, and re-layouts  1.67 us (2%)
    pallas_call x1, Pallas kernels, per_device(): pl.pallas_call(kernel, out_shape=jax.ShapeDtypeStruct((2, 2, 4, 16, 256),...  81.1 us
    unnamed x1, local copies, waits for them, and re-layouts  1.67 us

profile of v2, /device:TPU:1, one launch (start us, length us, event | category | flops | bytes accessed | tf_op | source)
XLA Modules:
  0.0 82.7 jit_solution(18253557278174592827)
XLA Ops:
  0.0 81.1 %shard_map.91 = f32[2,2,4,16,256]{4,3,2,1,0:T(8,128)} custom-call(s32[4,16,256]{2,1,0:T(8,128)} %labels_hbm.1, f32[1,8]{1,0:T(1,128)} %bitcast.4, f32[1,8]{1,0:T(1,128)} %bitcast.5, f32[2,2,16]{2,1,0:T(2,128)} %bitcast.3, s32[2,16]{1,0:T(2,128)} %sx_hbm.1, s32[2,16]{1,0:T(2,128)} %sy_hbm.1, s32[2,16]{1,0:T(2,128)} %sz_hbm.1, ...), custom_call_target="tpu_custom_call" | custom-call | tf_op jit(solution)/shard_map/pallas_call | solution.py:368
  81.1 1.7 %copy.11 = f32[2,2,4,16,256]{4,3,2,1,0:T(8,128)} copy(f32[2,2,4,16,256]{4,3,2,1,0:T(8,128)} %shard_map.91) | data formatting | bytes 524288

commit v3 on v2

--- a/solution.py
+++ b/solution.py
@@ -128,7 +128,11 @@
 
 def farthest_first():
     offsets = [(y, x, z) for y in range(4) for x in range(4) for z in range(8)][1:]
-    return sorted(offsets, key=lambda o: -(min(o[0], 4 - o[0]) + min(o[1], 4 - o[1]) + min(o[2], 8 - o[2])))
+
+    def hops(step, size):
+        return min(step, size - step)
+
+    return sorted(offsets, key=lambda o: (-(hops(o[0], 4) + hops(o[1], 4) + hops(o[2], 8)), hops(o[2], 8)))
 
 
 def kernel(
@@ -222,6 +226,10 @@
 
     def below(v):
         return jnp.concatenate(v, axis=0)
+
+    def to_space(v):
+        v = cmul_conj(sides(matmul(split(beside(v)), weights(5))), turns(1))
+        return matmul(weights(3), split(below(v)))
 
     for load in loads[1:8]:
         load.wait()
@@ -253,6 +261,8 @@
     first[...] = jnp.zeros_like(first)
     loads[0].wait()
     loads[8].wait()
+    for p in range(2):
+        send[BACK, p] = to_space(sides(spectrum[p]))
     for x in range(4):
         edge[x : x + 1] = labels[4 * core + x, 0:1]
         edge[4 + x : 5 + x] = labels[4 * core + x, 15:16]
@@ -301,11 +311,10 @@
                 arrived(OUT, p)
                 v = cmul(halves(matmul(weights(2), split(recv[OUT, p]))), turns(1))
                 v = sides(matmul(split(beside(v)), weights(4)))
-                spectrum[p] = beside(cmul(v, (green[p, 0], green[p, 1])))
+                v = to_space(cmul(v, (green[p, 0], green[p, 1])))
                 sent(BACK, p)
-
-            v = cmul_conj(sides(matmul(split(spectrum[p]), weights(5))), turns(1))
-            send[BACK, p] = matmul(weights(3), split(below(v)))
+                send[BACK, p] = v
+
             start(BACK, p)
 
         @pl.when(step == 0)
@@ -400,9 +409,9 @@
             dma,
         ],
         compiler_params=pltpu.CompilerParams(
-            collective_id=0, has_side_effects=True, vmem_limit_bytes=56 * 1024 * 1024
+            collective_id=0, has_side_effects=True, vmem_limit_bytes=32 * 1024 * 1024
         ),
-    )(
+    )(*(pltpu.with_memory_space_constraint(a, pltpu.HBM) for a in (
         labels,
         speed.reshape(1, 8),
         absorption.reshape(1, 8),
@@ -412,7 +421,7 @@
         source_z,
         jnp.asarray(transform_matrices()),
         jnp.asarray(constant_tables()),
-    )
+    )))
 
 
 def solution(mesh):

time: 82.9 us -> 79.4 us (0.958)
  Pallas kernels: 81.1 us -> 78.6 us
  local copies, waits for them, and re-layouts: 1.67 us -> 0.71 us
    pallas_call x1, Pallas kernels: 81.1 us -> 78.6 us  [per_device(): pl.pallas_call(kernel, out_shape=jax.ShapeDtypeStruct((2, 2, 4, 16, 256),...]
    unnamed x1, local copies, waits for them, and re-layouts: 1.67 us -> 0.71 us
where the time goes in v3:
time: 79.4 us; the launch traced here: 79.3 us
  Pallas kernels  78.6 us (99%)
    pallas_call x1, Pallas kernels, per_device(): pl.pallas_call(kernel, out_shape=jax.ShapeDtypeStruct((2, 2, 4, 16, 256),...  78.6 us

profile of v3, /device:TPU:1, one launch (start us, length us, event | category | flops | bytes accessed | tf_op | source)
XLA Modules:
  0.0 79.3 jit_solution(2014359409459527426)
XLA Ops:
  0.0 78.6 %shard_map.91 = f32[2,2,4,16,256]{4,3,2,1,0:T(8,128)S(1)} custom-call(s32[4,16,256]{2,1,0:T(8,128)} %labels_hbm.1, f32[1,8]{1,0:T(1,128)} %bitcast.4, f32[1,8]{1,0:T(1,128)} %bitcast.5, f32[2,2,16]{2,1,0:T(2,128)} %bitcast.3, s32[2,16]{1,0:T(2,128)} %sx_hbm.1, s32[2,16]{1,0:T(2,128)} %sy_hbm.1, s32[2,16]{1,0:T(2,128)} %sz_hbm.1, ...), custom_call_target="tpu_custom_call" | custom-call | tf_op jit(solution)/shard_map/pallas_call | solution.py:377
  78.6 0.7 copy.11

commit v4 on v3

--- a/solution.py
+++ b/solution.py
@@ -274,20 +274,19 @@
             device_id=device, device_id_type=MESH,
         )
 
+    own = labels.at[pl.ds(4 * core, 4)]
+    beside_x = lax.rem(chip_x + 7 + 2 * core, 8)
+    copies = [to_others(0, own, own, 0, (sibling, gy))]
+    for c in range(2):
+        copies.append(
+            to_others(1 + c, labels.at[7 * core], near_x.at[1 - core], 2 - core, (2 * beside_x + c, gy))
+        )
+        for d, to in enumerate((next_y, last_y)):
+            copies.append(
+                to_others(3 + 2 * d + c, edge, near_y.at[d, core], 3 + 2 * d + core, (2 * chip_x + c, to))
+            )
+
     def medium_of_cells():
-        own = labels.at[pl.ds(4 * core, 4)]
-        beside_x = lax.rem(chip_x + 7 + 2 * core, 8)
-        copies = [to_others(0, own, own, 0, (sibling, gy))]
-        for c in range(2):
-            copies.append(
-                to_others(1 + c, labels.at[7 * core], near_x.at[1 - core], 2 - core, (2 * beside_x + c, gy))
-            )
-            for d, to in enumerate((next_y, last_y)):
-                copies.append(
-                    to_others(3 + 2 * d + c, edge, near_y.at[d, core], 3 + 2 * d + core, (2 * chip_x + c, to))
-                )
-        for copy in copies:
-            copy.start()
         theirs = labels.at[pl.ds(4 - 4 * core, 4)]
         landed = [theirs, near_x.at[0], near_x.at[1]] + [near_y.at[d, c] for d in range(2) for c in range(2)]
         for k, ref in enumerate(landed):
@@ -316,6 +315,13 @@
                 send[BACK, p] = v
 
             start(BACK, p)
+            if p == 0:
+
+                @pl.when(step == 0)
+                def _():
+                    for copy in copies:
+                        copy.start()
+
 
         @pl.when(step == 0)
         def _():
@@ -355,20 +361,26 @@
 
     lax.fori_loop(0, ITERS, iteration, 0)
 
+    copies = []
     for part in range(2):
         result[part] = beside((field[part, 0:128].T, field[part, 128:256].T)).reshape(8, 16, 256)
-    theirs = pltpu.make_async_remote_copy(
-        src_ref=result.at[:, pl.ds(4 - 4 * core, 4)], dst_ref=out.at[core], send_sem=half_send, recv_sem=half_recv,
-        device_id=(sibling, gy), device_id_type=MESH,
-    )
-    theirs.start()
-    out[core] = result[:, pl.ds(4 * core, 4)]
-    landed = out.at[1 - core]
-    pltpu.make_async_copy(landed, landed, half_recv).wait()
-    theirs.wait_send()
+        copies.append(
+            pltpu.make_async_remote_copy(
+                src_ref=result.at[part, pl.ds(4 - 4 * core, 4)], dst_ref=out.at[core, part],
+                send_sem=half_send.at[part], recv_sem=half_recv.at[part],
+                device_id=(sibling, gy), device_id_type=MESH,
+            )
+        )
+        copies[part].start()
+    for part in range(2):
+        out[core, part] = result[part, pl.ds(4 * core, 4)]
     for stage in range(2):
         for p in range(2):
             sent(stage, p)
+    for part in range(2):
+        landed = out.at[1 - core, part]
+        pltpu.make_async_copy(landed, landed, half_recv.at[part]).wait()
+        copies[part].wait_send()
 
 
 def per_device(labels, speed, absorption, amplitude, source_x, source_y, source_z):
@@ -405,8 +417,8 @@
             dma((2, 2)),
             dma((7,)),
             dma((7,)),
-            dma,
-            dma,
+            dma((2,)),
+            dma((2,)),
         ],
         compiler_params=pltpu.CompilerParams(
             collective_id=0, has_side_effects=True, vmem_limit_bytes=32 * 1024 * 1024

time: 79.4 us -> 78.6 us (0.990)
  Pallas kernels: 78.6 us -> 77.8 us
    pallas_call x1, Pallas kernels: 78.6 us -> 77.8 us  [per_device(): pl.pallas_call(kernel, out_shape=jax.ShapeDtypeStruct((2, 2, 4, 16, 256),...]
where the time goes in v4:
time: 78.6 us; the launch traced here: 78.5 us
  Pallas kernels  77.8 us (99%)
    pallas_call x1, Pallas kernels, per_device(): pl.pallas_call(kernel, out_shape=jax.ShapeDtypeStruct((2, 2, 4, 16, 256),...  77.8 us

profile of v4, /device:TPU:1, one launch (start us, length us, event | category | flops | bytes accessed | tf_op | source)
XLA Modules:
  0.0 78.5 jit_solution(8778806103523278888)
XLA Ops:
  0.0 77.8 %shard_map.91 = f32[2,2,4,16,256]{4,3,2,1,0:T(8,128)S(1)} custom-call(s32[4,16,256]{2,1,0:T(8,128)} %labels_hbm.1, f32[1,8]{1,0:T(1,128)} %bitcast.4, f32[1,8]{1,0:T(1,128)} %bitcast.5, f32[2,2,16]{2,1,0:T(2,128)} %bitcast.3, s32[2,16]{1,0:T(2,128)} %sx_hbm.1, s32[2,16]{1,0:T(2,128)} %sy_hbm.1, s32[2,16]{1,0:T(2,128)} %sz_hbm.1, ...), custom_call_target="tpu_custom_call" | custom-call | tf_op jit(solution)/shard_map/pallas_call | solution.py:389
  77.8 0.7 copy.11

commit v5 on v4

--- a/solution.py
+++ b/solution.py
@@ -132,7 +132,7 @@
     def hops(step, size):
         return min(step, size - step)
 
-    return sorted(offsets, key=lambda o: (-(hops(o[0], 4) + hops(o[1], 4) + hops(o[2], 8)), hops(o[2], 8)))
+    return sorted(offsets, key=lambda o: (-(hops(o[0], 4) + hops(o[1], 4) + hops(o[2], 8)), hops(o[2], 8), hops(o[1], 4), o[0]))
 
 
 def kernel(
@@ -329,16 +329,18 @@
 
         arrived(BACK, 0)
         even = halves(matmul(weights(1), split(recv[BACK, 0])))
+        change = [below((even[k], even[k])) + first[k] - field[k] for k in range(2)]
+        moved = cmul((potential[0], potential[1]), change)
+        field[0], field[1] = field[0] - moved[1] * inverse, field[1] + moved[0] * inverse
         arrived(BACK, 1)
         odd = cmul_conj(halves(matmul(weights(1), split(recv[BACK, 1]))), turns(0))
-        scattered = [below((even[k] + odd[k], even[k] - odd[k])) for k in range(2)]
-        change = [scattered[k] + first[k] - field[k] for k in range(2)]
-        moved = cmul((potential[0], potential[1]), change)
+        odd = [below((odd[k], -odd[k])) for k in range(2)]
+        moved = cmul((potential[0], potential[1]), odd)
         field[0], field[1] = field[0] - moved[1] * inverse, field[1] + moved[0] * inverse
 
         @pl.when(step == 0)
         def _():
-            first[0], first[1] = scattered
+            first[0], first[1] = [below((even[k], even[k])) + odd[k] for k in range(2)]
 
         @pl.when(step < ITERS - 1)
         def _():

time: 78.6 us -> 78.4 us (level)
  no operation moved by 1% of the time
where the time goes in v5:
time: 78.4 us
  Pallas kernels  77.7 us (99%)
    pallas_call x1, Pallas kernels, per_device(): pl.pallas_call(kernel, out_shape=jax.ShapeDtypeStruct((2, 2, 4, 16, 256),...  77.7 us

profile of v5, /device:TPU:1, one launch (start us, length us, event | category | flops | bytes accessed | tf_op | source)
XLA Modules:
  0.0 78.4 jit_solution(7663587940212863579)
XLA Ops:
  0.0 77.7 %shard_map.91 = f32[2,2,4,16,256]{4,3,2,1,0:T(8,128)S(1)} custom-call(s32[4,16,256]{2,1,0:T(8,128)} %labels_hbm.1, f32[1,8]{1,0:T(1,128)} %bitcast.4, f32[1,8]{1,0:T(1,128)} %bitcast.5, f32[2,2,16]{2,1,0:T(2,128)} %bitcast.3, s32[2,16]{1,0:T(2,128)} %sx_hbm.1, s32[2,16]{1,0:T(2,128)} %sy_hbm.1, s32[2,16]{1,0:T(2,128)} %sz_hbm.1, ...), custom_call_target="tpu_custom_call" | custom-call | tf_op jit(solution)/shard_map/pallas_call | solution.py:391
  77.7 0.7 copy.11
